TPU v7x, 32 devices: a whole 2x2x4 slice. The times are simulated.
32 devices in a mesh: row: 4 (over z), col: 8 (over y, x, core).
Axes of the slice: x: 2, y: 2, z: 4, core: 2. Of those that a mesh axis runs over, the one named last changes fastest.
Arguments:
- panel_first: bfloat16 [32, 256, 1024], P(('row', 'col')), may hold values from -3 to 3
- panel_second: bfloat16 [32, 256, 1024], P(('row', 'col')), may hold values from -4 to 4
- diag_first: bfloat16 [1024, 1024], P('col'), as said below
- bridge: bfloat16 [1024, 1024], P('col'), may hold values from -0.024902344 to 0.024902344
- diag_second: bfloat16 [1024, 1024], P('col'), as said below
- trailing: float32 [32, 24, 256, 256], P(('row', 'col')), may hold values from -6 to 6
- trail_pairs: int32 [32, 2, 24], P(('row', 'col')), may hold values from 0 to 7, as said below
- live_count: int32 [32], P(('row', 'col')), may hold values from 1 to 24, as said below
Outputs:
- lower_first: bfloat16 [32, 256, 1024], P(('row', 'col'))
- lower_second: bfloat16 [32, 256, 1024], P(('row', 'col'))
- trailing_out: float32 [32, 24, 256, 256], P(('row', 'col'))
Inputs may be any that keep to these rules, and one draw needn't show every extreme that they name: `trail_pairs`: on each device the listed pairs are distinct; the first entry of a pair is below 8 and the second below 4. `live_count`: some device has all 24 slots live in every draw. `diag_first`: symmetric and positive definite, with diagonal entries between 0.75 and 2.3. `diag_second`: symmetric and positive definite, with diagonal entries between 3.4 and 7.5.
All inputs are finite; a program needn't handle non-finite values.
Results may differ from a plain program's by a relative error of at most 0.001.
Values may be sent and summed in bfloat16 or wider, within the bound.
A program may use at most 192 MiB of HBM per device.

v0:
```python
import jax
import jax.numpy as jnp
from jax import lax
from jax.sharding import PartitionSpec as P


def right_solve(lower_factor, block_rows):
    return jax.scipy.linalg.solve_triangular(lower_factor, block_rows.T, lower=True).T


def tile_product(left_tile, right_tile):
    return lax.dot_general(
        left_tile, right_tile, (((1,), (1,)), ((), ())), preferred_element_type=jnp.float32
    )


def apply_owned(trailing, row_tiles, col_tiles, pair_list, first_slot, stop_slot):

    def step_index(slot_index, carried):
        update = tile_product(
            row_tiles[pair_list[0, slot_index]], col_tiles[pair_list[1, slot_index]]
        )
        current = lax.dynamic_index_in_dim(carried, slot_index, 0, keepdims=False)
        return lax.dynamic_update_index_in_dim(carried, current - update, slot_index, 0)

    return lax.fori_loop(first_slot, stop_slot, step_index, trailing)


def update_tiles(trailing, row_tiles, col_tiles, pair_list, live_slots):
    return apply_owned(trailing, row_tiles, col_tiles, pair_list, 0, live_slots)


def per_device(
    panel_first, panel_second, diag_first, bridge, diag_second, trailing, trail_pairs, live_count
):
    highest = lax.Precision.HIGHEST
    whole_first, whole_bridge, whole_second = (
        lax.all_gather(diag_first, "col", axis=0, tiled=True),
        lax.all_gather(bridge, "col", axis=0, tiled=True),
        lax.all_gather(diag_second, "col", axis=0, tiled=True),
    )
    factor_first = jnp.linalg.cholesky(whole_first.astype(jnp.float32))
    coupling = right_solve(factor_first, whole_bridge.astype(jnp.float32))
    shifted = whole_second.astype(jnp.float32) - jnp.dot(
        coupling, coupling.T, precision=highest, preferred_element_type=jnp.float32
    )
    factor_second = jnp.linalg.cholesky(shifted)
    lower_first = right_solve(factor_first, panel_first[0].astype(jnp.float32)).astype(jnp.bfloat16)
    pair_list = trail_pairs[0]
    live_slots = live_count[0]
    owned = trailing[0]
    reduced = panel_second[0].astype(jnp.float32) - jnp.dot(
        lower_first.astype(jnp.float32),
        coupling.T,
        precision=highest,
        preferred_element_type=jnp.float32,
    )
    lower_second = right_solve(factor_second, reduced).astype(jnp.bfloat16)
    joined_tiles = jnp.concatenate([lower_first, lower_second], axis=1)[None]
    row_tiles = lax.all_gather(joined_tiles, "col", axis=0, tiled=True)
    col_tiles = lax.all_gather(joined_tiles, "row", axis=0, tiled=True)
    owned = update_tiles(owned, row_tiles, col_tiles, pair_list, live_slots)
    return (lower_first[None], lower_second[None], owned[None])


def solution(mesh):
    return jax.shard_map(
        per_device,
        mesh=mesh,
        in_specs=(
            P(("row", "col"), None, None),
            P(("row", "col"), None, None),
            P("col", None),
            P("col", None),
            P("col", None),
            P(("row", "col"), None, None, None),
            P(("row", "col"), None, None),
            P(("row", "col")),
        ),
        out_specs=(
            P(("row", "col"), None, None),
            P(("row", "col"), None, None),
            P(("row", "col"), None, None, None),
        ),
        check_vma=False,
    )
```

profile of v0, /device:TPU:15, one launch (start us, length us, event | category | flops | bytes accessed | tf_op | source)
XLA Modules:
  0.0 1150.3 jit_solution(15925453633398445978)
XLA Ops:
  7.2 6.2 copy.141
  16.2 27.1 %all-gather.8.cloned.1.call-done = bf16[1024,1024]{0,1:T(8,128)(2,1)} async-done(((bf16[128,1024]{0,1:T(8,128)(2,1)}), bf16[1024,1024]{0,1:T(8,128)(2,1)}) %all-gather.8.cloned.1.call-update) | async-done | bytes 2097168 | tf_op jit(solution)/shard_map/all_gather | solution.py:38
  43.2 4.3 copy.12
  47.5 2.9 fusion.8
  52.3 11.7 %cholesky.619 = f32[128,128]{1,0:T(8,128)S(1)} custom-call(f32[128,128]{1,0:T(8,128)S(1)} %cholesky.911), custom_call_target="Cholesky" | custom-call | tf_op jit(solution)/shard_map/jit(cholesky)/cholesky | solution.py:42
  64.1 9.8 custom-call.60
  80.3 11.7 %cholesky.638 = f32[128,128]{1,0:T(8,128)S(1)} custom-call(f32[128,128]{1,0:T(8,128)S(1)} %cholesky.915), custom_call_target="Cholesky" | custom-call | tf_op jit(solution)/shard_map/jit(cholesky)/cholesky | solution.py:42
  92.7 10.1 custom-call.61
  106.2 11.7 %cholesky.659 = f32[128,128]{1,0:T(8,128)S(1)} custom-call(f32[128,128]{1,0:T(8,128)S(1)} %cholesky.920), custom_call_target="Cholesky" | custom-call | tf_op jit(solution)/shard_map/jit(cholesky)/cholesky | solution.py:42
  119.2 9.8 custom-call.62
  132.5 11.9 %cholesky.678 = f32[128,128]{1,0:T(8,128)S(1)} custom-call(f32[128,128]{1,0:T(8,128)S(1)} %cholesky.925), custom_call_target="Cholesky" | custom-call | tf_op jit(solution)/shard_map/jit(cholesky)/cholesky | solution.py:42
  145.6 9.8 custom-call.63
  158.9 11.7 %cholesky.697 = f32[128,128]{1,0:T(8,128)S(1)} custom-call(f32[128,128]{1,0:T(8,128)S(1)} %cholesky.930), custom_call_target="Cholesky" | custom-call | tf_op jit(solution)/shard_map/jit(cholesky)/cholesky | solution.py:42
  171.9 9.8 custom-call.64
  185.3 11.7 %cholesky.716 = f32[128,128]{1,0:T(8,128)S(1)} custom-call(f32[128,128]{1,0:T(8,128)S(1)} %cholesky.935), custom_call_target="Cholesky" | custom-call | tf_op jit(solution)/shard_map/jit(cholesky)/cholesky | solution.py:42
  198.2 9.8 custom-call.65
  211.0 11.7 %cholesky.735 = f32[128,128]{1,0:T(8,128)S(1)} custom-call(f32[128,128]{1,0:T(8,128)S(1)} %cholesky.940), custom_call_target="Cholesky" | custom-call | tf_op jit(solution)/shard_map/jit(cholesky)/cholesky | solution.py:42
  224.1 10.2 custom-call.66
  236.9 11.7 %cholesky.752 = f32[128,128]{1,0:T(8,128)S(1)} custom-call(f32[128,128]{1,0:T(8,128)S(1)} %convolution_subtract_fusion.34), custom_call_target="Cholesky" | custom-call | tf_op jit(solution)/shard_map/jit(cholesky)/cholesky | solution.py:42
  255.5 4.8 select_select_fusion.1
  260.4 23.1 %while.16 = (s32[]{:T(128)}, f32[1024,1024]{1,0:T(8,128)}, s32[8,2]{0,1:T(2,128)S(1)}, f32[8,128,128]{2,1,0:T(8,128)S(1)}, s32[]{:T(128)}) while((s32[]{:T(128)}, f32[1024,1024]{1,0:T(8,128)}, s32[8,2]{0,1:T(2,128)S(1)}, f32[8,128,128]{2,1,0:T(8,128)S(1)}, s32[]{:T(128)}) %tuple.158), condition=%wide.while_cond, body=%wide.while_body.sunk | while | flops 2 | bytes 131181 | solution.py:8
  283.5 78.8 %custom-call.67 = f32[8,128,128]{1,2,0:T(8,128)S(1)} custom-call(f32[8,128,128]{2,1,0:T(8,128)S(1)} %get-tuple-element.61), custom_call_target="InvertDiagBlocksLowerTriangular" | custom-call | tf_op jit(solution)/shard_map/jit(_solve_triangular)/triangular_solve | solution.py:8
  368.7 2.7 convolution_subtract_fusion.2
  373.0 3.7 fusion.24
  378.3 4.4 fusion.27
  384.7 5.4 convolution_subtract_fusion.4
  391.6 6.1 convolution_subtract_fusion.3
  399.2 7.3 convolution_subtract_fusion.5
  407.9 18.1 %convert_subtract_fusion = f32[1024,1024]{0,1:T(8,128)} fusion(bf16[1024,1024]{0,1:T(8,128)(2,1)} %all-gather.10.cloned.1.call-done, f32[1024,1024]{1,0:T(8,128)} %convolution_dynamic-update-slice_fusion), kind=kOutput, calls=%fused_computation.22 | convolution fusion | flops 12886999040 | bytes 10485760 | tf_op jit(solution)/shard_map/dot_general | solution.py:44
  426.1 5.7 copy.15
  431.8 4.4 fusion.7
  438.2 11.7 %cholesky.767 = f32[128,128]{1,0:T(8,128)S(1)} custom-call(f32[128,128]{1,0:T(8,128)S(1)} %cholesky.944), custom_call_target="Cholesky" | custom-call | tf_op jit(solution)/shard_map/jit(cholesky)/cholesky | solution.py:47
  452.5 9.8 custom-call.68
  466.2 11.9 %cholesky.786 = f32[128,128]{1,0:T(8,128)S(1)} custom-call(f32[128,128]{1,0:T(8,128)S(1)} %cholesky.948), custom_call_target="Cholesky" | custom-call | tf_op jit(solution)/shard_map/jit(cholesky)/cholesky | solution.py:47
  480.0 9.8 custom-call.69
  493.2 11.7 %cholesky.807 = f32[128,128]{1,0:T(8,128)S(1)} custom-call(f32[128,128]{1,0:T(8,128)S(1)} %cholesky.953), custom_call_target="Cholesky" | custom-call | tf_op jit(solution)/shard_map/jit(cholesky)/cholesky | solution.py:47
  506.3 9.8 custom-call.70
  519.6 11.9 %cholesky.826 = f32[128,128]{1,0:T(8,128)S(1)} custom-call(f32[128,128]{1,0:T(8,128)S(1)} %cholesky.958), custom_call_target="Cholesky" | custom-call | tf_op jit(solution)/shard_map/jit(cholesky)/cholesky | solution.py:47
  532.9 9.8 custom-call.71
  546.1 11.7 %cholesky.845 = f32[128,128]{1,0:T(8,128)S(1)} custom-call(f32[128,128]{1,0:T(8,128)S(1)} %cholesky.963), custom_call_target="Cholesky" | custom-call | tf_op jit(solution)/shard_map/jit(cholesky)/cholesky | solution.py:47
  559.1 10.2 custom-call.72
  572.6 11.7 %cholesky.864 = f32[128,128]{1,0:T(8,128)S(1)} custom-call(f32[128,128]{1,0:T(8,128)S(1)} %cholesky.968), custom_call_target="Cholesky" | custom-call | tf_op jit(solution)/shard_map/jit(cholesky)/cholesky | solution.py:47
  585.6 9.8 custom-call.73
  598.4 11.9 %cholesky.883 = f32[128,128]{1,0:T(8,128)S(1)} custom-call(f32[128,128]{1,0:T(8,128)S(1)} %cholesky.973), custom_call_target="Cholesky" | custom-call | tf_op jit(solution)/shard_map/jit(cholesky)/cholesky | solution.py:47
  611.6 9.8 custom-call.74
  624.0 11.7 %cholesky.900 = f32[128,128]{1,0:T(8,128)S(1)} custom-call(f32[128,128]{1,0:T(8,128)S(1)} %convolution_subtract_fusion.33), custom_call_target="Cholesky" | custom-call | tf_op jit(solution)/shard_map/jit(cholesky)/cholesky | solution.py:47
  642.1 4.8 select_select_fusion
  647.0 23.2 %while.17 = (s32[]{:T(128)}, f32[1024,1024]{1,0:T(8,128)}, s32[8,2]{0,1:T(2,128)S(1)}, f32[8,128,128]{2,1,0:T(8,128)S(1)}, s32[]{:T(128)}) while((s32[]{:T(128)}, f32[1024,1024]{1,0:T(8,128)}, s32[8,2]{0,1:T(2,128)S(1)}, f32[8,128,128]{2,1,0:T(8,128)S(1)}, s32[]{:T(128)}) %tuple.180), condition=%wide.while_cond.clone, body=%wide.while_body.clone.sunk | while | flops 2 | bytes 131181 | solution.py:8
  670.2 79.4 %custom-call.75 = f32[8,128,128]{1,2,0:T(8,128)} custom-call(f32[8,128,128]{2,1,0:T(8,128)S(1)} %get-tuple-element.62), custom_call_target="InvertDiagBlocksLowerTriangular" | custom-call | tf_op jit(solution)/shard_map/jit(_solve_triangular)/triangular_solve | solution.py:8
  766.0 4.4 fusion.23
  790.8 75.9 %all-gather.16.cloned.1.call-done = bf16[1024,2048]{0,1:T(8,128)(2,1)} async-done(((bf16[256,2048]{0,1:T(8,128)(2,1)}), bf16[1024,2048]{0,1:T(8,128)(2,1)}) %all-gather.16.cloned.1.call-update) | async-done | bytes 4194320 | tf_op jit(solution)/shard_map/all_gather | solution.py:61
  866.6 6.5 copy.22
  873.1 51.7 %all-gather.14.cloned.1.call-done = bf16[2048,2048]{0,1:T(8,128)(2,1)} async-done(((bf16[256,2048]{0,1:T(8,128)(2,1)}), bf16[2048,2048]{0,1:T(8,128)(2,1)}) %all-gather.14.cloned.1.call-update) | async-done | bytes 8388624 | tf_op jit(solution)/shard_map/all_gather | solution.py:60
  924.8 12.3 %copy.21 = bf16[2048,2048]{1,0:T(8,128)(2,1)} copy(bf16[2048,2048]{0,1:T(8,128)(2,1)} %all-gather.14.cloned.1.call-done) | data formatting | bytes 16777216 | tf_op jit(solution)/shard_map/while | solution.py:26
  937.1 206.2 %while.15 = (s32[]{:T(128)}, f32[24,256,256]{2,1,0:T(8,128)}, s32[]{:T(128)}, s32[2,24]{1,0:T(2,128)S(1)}, bf16[8,256,2048]{2,1,0:T(8,128)(2,1)}, /*index=5*/bf1...) while((s32[]{:T(128)}, f32[24,256,256]{2,1,0:T(8,128)}, ...), condition=%wide.region_17.20_spmd, body=%wide.region_16.19_spmd.sunk | while | flops 268500992 | bytes 3145975 | solution.py:26
  960.1 2.7 fusion.220
  968.6 2.7 fusion.220
  977.2 2.7 fusion.220
  985.8 2.7 fusion.220
  1002.9 2.7 fusion.220
  1020.0 2.7 fusion.220
  1037.2 2.7 fusion.220
  1054.3 2.7 fusion.220
  1071.4 2.7 fusion.220
  (268 shorter events, 254.2 us)
Async XLA Ops:
  7.2 6.3 copy-start.7
  7.2 8.9 copy-start.4
  7.2 7.9 copy-start.8
  7.2 36.0 %all-gather.8.cloned.1.call-start = ((), (), s32[]{:S(2)}) async-start(), calls=%async_computation | async-start | bytes 2359296 | tf_op jit(solution)/shard_map/all_gather | solution.py:38
  14.3 348.0 %all-gather.12.cloned.1.call-start = ((), (), s32[]{:S(2)}) async-start(), calls=%async_computation.2 | async-start | bytes 2359296 | tf_op jit(solution)/shard_map/all_gather | solution.py:39
  15.0 392.9 %all-gather.10.cloned.1.call-start = ((), (), s32[]{:S(2)}) async-start(), calls=%async_computation.1 | async-start | bytes 2359296 | tf_op jit(solution)/shard_map/all_gather | solution.py:40
  16.0 850.7 %all-gather.16.cloned.1.call-start = ((), (), s32[]{:S(2)}) async-start(), calls=%async_computation.4 | async-start | bytes 5242880 | tf_op jit(solution)/shard_map/all_gather | solution.py:61
  43.2 4.3 copy-start.2
  50.4 1.9 copy-start.1
  362.3 2.5 copy-start.3
  436.3 2.0 copy-start
  755.1 10.9 copy-start.5
  763.0 7.5 copy-start.6
  788.2 136.6 %all-gather.14.cloned.1.call-start = ((), (), s32[]{:S(2)}) async-start(), calls=%async_computation.3 | async-start | bytes 9437184 | tf_op jit(solution)/shard_map/all_gather | solution.py:60
  873.1 64.0 %copy-start.9 = (s32[1,2,24]{2,1,0:T(2,128)S(1)}, s32[1,2,24]{2,1,0:T(2,128)}, u32[]{:S(2)}) copy-start(s32[1,2,24]{2,1,0:T(2,128)} %param.19) | copy-start | bytes 580
Sparse Core Ops, SparseCore 0:
  14.4 28.7 all-gather.7
  45.1 27.9 all-gather.11
  75.6 28.7 all-gather.9
  788.3 78.3 all-gather.15
  868.4 56.3 all-gather.13
where the time goes:
time: 1170 us; the launch traced here: 1150 us
  other arithmetic  522 us (45%)
  matrix products  212 us (18%)
  waiting for transfers between devices  156 us (13%)
  local copies, waits for them, and re-layouts  132 us (11%)
  loops' own time  103 us (9%)
  between operations  25 us (2%)
    another operation x31, other arithmetic, per_device(): factor_second = jnp.linalg.cholesky(shifted)  173 us
    another operation x30, other arithmetic, per_device(): factor_first = jnp.linalg.cholesky(whole_first.astype(jnp.float32))  172 us
    another operation x5, other arithmetic, right_solve(): jax.scipy.linalg.solve_triangular(lower_factor, block_rows.T, lower=True)  168 us
    another operation x1, loops' own time, apply_owned(): return lax.fori_loop(first_slot, stop_slot, step_index, trailing)  103 us
    another operation x45, matrix products, right_solve(): jax.scipy.linalg.solve_triangular(lower_factor, block_rows.T, lower=True)  77.9 us
    all_gather x1, waiting for transfers between devices, per_device(): col_tiles = lax.all_gather(joined_tiles, 'row', axis=0, tiled=True)  75.9 us
    dot_general x24, matrix products, tile_product(): lax.dot_general(left_tile, right_tile, (((1,), (1,)), ((), ())), preferre...  65.5 us
    all_gather x1, waiting for transfers between devices, per_device(): row_tiles = lax.all_gather(joined_tiles, 'col', axis=0, tiled=True)  51.7 us
  transfers between devices with their start and end apart: 5, of which 3 were waited for; matrix products, arithmetic and copies ran while one was open for 32% of the time, Pallas kernels for 0%

commit v1 on v0

v1 whole, which is shorter than its diff:
```python
import functools

import jax
import jax.numpy as jnp
from jax import lax
from jax.experimental import pallas as pl
from jax.experimental.pallas import tpu as pltpu
from jax.sharding import PartitionSpec as P

BLOCK = 128
MICRO = 16
HALF = 8
F32 = jnp.float32
BF16 = jnp.bfloat16


def split_outside(x):
    high = lax.reduce_precision(x, 8, 7)
    return high.astype(BF16), (x - high).astype(BF16)


def split2(x):
    high = x.astype(BF16)
    return high, (x - high.astype(F32)).astype(BF16)


def split3(x):
    high = x.astype(BF16)
    rest = x - high.astype(F32)
    mid = rest.astype(BF16)
    return high, mid, (rest - mid.astype(F32)).astype(BF16)


def dot_tn(left, right):
    return lax.dot_general(left, right, (((0,), (0,)), ((), ())), preferred_element_type=F32)


def dot_nn(left, right):
    return lax.dot_general(left, right, (((1,), (0,)), ((), ())), preferred_element_type=F32)


def dot_nt(left, right):
    return lax.dot_general(left, right, (((1,), (1,)), ((), ())), preferred_element_type=F32)


def inverse_factor_block(block):
    rows = lax.broadcasted_iota(jnp.int32, (HALF, BLOCK), 0)
    row = lax.broadcasted_iota(jnp.int32, (BLOCK, BLOCK), 0)
    column = lax.broadcasted_iota(jnp.int32, (BLOCK, BLOCK), 1)
    left = block
    right = jnp.where(row == column, 1.0, 0.0).astype(F32)
    done = []
    for first in range(0, BLOCK, MICRO):
        last = first + MICRO
        here = left[:MICRO]
        pieces = [
            [here[h : h + HALF] for h in range(0, MICRO, HALF)],
            [right[h : h + HALF] for h in range(0, MICRO, HALF)],
        ]
        columns = [
            [
                jnp.broadcast_to(piece[:, first + k : first + k + 1], (HALF, BLOCK))
                for piece in pieces[0]
            ]
            for k in range(MICRO)
        ]
        pivots = [jnp.ones((HALF, BLOCK), F32) for _ in range(MICRO // HALF)]
        for i in range(MICRO):
            part, within = divmod(i, HALF)
            pivot = jnp.broadcast_to(columns[i][part][within : within + 1], (HALF, BLOCK))
            pivots[part] = jnp.where(rows == within, pivot, pivots[part])
            inverse = 1.0 / pivot
            factors = {}
            for other in range(part, MICRO // HALF):
                below = columns[i][other]
                if other == part:
                    below = jnp.where(rows > within, below, 0.0)
                factors[other] = below * inverse
            for held in pieces + columns[i + 1 :]:
                source = jnp.broadcast_to(held[part][within : within + 1], (HALF, BLOCK))
                for other in range(part, MICRO // HALF):
                    held[other] = held[other] - factors[other] * source
        scales = [lax.rsqrt(pivot) for pivot in pivots]
        upper = jnp.concatenate([a * s for a, s in zip(pieces[0], scales)], axis=0)
        inner = jnp.concatenate([a * s for a, s in zip(pieces[1], scales)], axis=0)
        done.append(inner)
        if last < BLOCK:
            uh, um, ul = split3(upper)
            wh, wm, wl = split3(inner)
            lhs = jnp.concatenate([uh, uh, um, um, uh, ul], axis=0)
            rhs_u = jnp.concatenate([uh, um, uh, um, ul, uh], axis=0)
            rhs_w = jnp.concatenate([wh, wm, wh, wm, wl, wh], axis=0)
            update_u = dot_tn(lhs, rhs_u)
            update_w = dot_tn(lhs, rhs_w)
            left = left[MICRO:] - update_u[last:]
            right = right[MICRO:] - update_w[last:]
    return jnp.concatenate(done, axis=0)


def factor_kernel(a_ref, high_ref, low_ref, grid_ref, terms_ref, flipped_ref):
    size = a_ref.shape[0]
    blocks = size // BLOCK
    grid_ref[...] = a_ref[...].astype(F32)

    @pl.loop(0, blocks)
    def _(k):
        here = pl.ds(pl.multiple_of(k * BLOCK, BLOCK), BLOCK)
        inverse = inverse_factor_block(grid_ref[here, here])
        grid_ref[here, here] = jnp.zeros((BLOCK, BLOCK), F32)
        inv_h, inv_l = split2(inverse)
        line_h, line_l = split2(grid_ref[here, :])
        grid_ref[here, :] = dot_nn(
            jnp.concatenate([inv_h, inv_h, inv_l], axis=1),
            jnp.concatenate([line_h, line_l, line_h], axis=0),
        )
        grid_ref[here, here] = inverse
        line_h, line_l = split2(grid_ref[here, :])
        terms_ref[...] = jnp.concatenate([line_h, line_l, line_h], axis=0)
        flipped_ref[...] = jnp.concatenate([line_h, line_h, line_l], axis=0)

        @pl.loop(k + 1, blocks)
        def _(i):
            below = pl.ds(pl.multiple_of(i * BLOCK, BLOCK), BLOCK)
            grid_ref[below, here] = jnp.zeros((BLOCK, BLOCK), F32)
            grid_ref[below, :] -= dot_tn(flipped_ref[:, below], terms_ref[...])

        column = lax.broadcasted_iota(jnp.int32, (BLOCK, size), 1)
        final = jnp.where(column < (k + 1) * BLOCK, grid_ref[here, :], 0.0)
        final_h, final_l = split2(final)
        high_ref[here, :] = final_h
        low_ref[here, :] = final_l


def inverse_factor(block):
    size = block.shape[0]
    whole = pl.BlockSpec(memory_space=pltpu.VMEM)
    return pl.pallas_call(
        factor_kernel,
        out_shape=[jax.ShapeDtypeStruct((size, size), BF16)] * 2,
        in_specs=[whole],
        out_specs=[whole, whole],
        scratch_shapes=[
            pltpu.VMEM((size, size), F32),
            pltpu.VMEM((3 * BLOCK, size), BF16),
            pltpu.VMEM((3 * BLOCK, size), BF16),
        ],
        compiler_params=pltpu.CompilerParams(vmem_limit_bytes=40 * 2**20),
        cost_estimate=pl.CostEstimate(flops=60 * 10**9, bytes_accessed=8 * 2**20, transcendentals=0),
        name="inverse_factor",
    )(block)


def trailing_kernel(pairs_ref, live_ref, row1_ref, row2_ref, col1_ref, col2_ref, in_ref, out_ref):
    slot = pl.program_id(0)

    @pl.when(slot < live_ref[0])
    def _():
        a = pairs_ref[0, slot]
        b = pairs_ref[1, slot]
        out_ref[0] = (
            in_ref[0] - dot_nt(row1_ref[a], col1_ref[b]) - dot_nt(row2_ref[a], col2_ref[b])
        )

    @pl.when(slot >= live_ref[0])
    def _():
        out_ref[0] = in_ref[0]


def trailing_update(pairs, live, row1, row2, col1, col2, trailing):
    slots, tile, _ = trailing.shape
    panel = row1.shape[-1]

    def whole(array):
        return pl.BlockSpec(array.shape, lambda s, *_: (0, 0, 0), pipeline_mode=pl.Buffered(1))

    one = pl.BlockSpec((1, tile, tile), lambda s, *_: (s, 0, 0))
    return pl.pallas_call(
        trailing_kernel,
        out_shape=jax.ShapeDtypeStruct(trailing.shape, F32),
        grid_spec=pltpu.PrefetchScalarGridSpec(
            num_scalar_prefetch=2,
            grid=(slots,),
            in_specs=[whole(row1), whole(row2), whole(col1), whole(col2), one],
            out_specs=one,
        ),
        compiler_params=pltpu.CompilerParams(vmem_limit_bytes=56 * 2**20),
        cost_estimate=pl.CostEstimate(
            flops=4 * slots * tile * tile * panel, bytes_accessed=30 * 2**20, transcendentals=0
        ),
        name="trailing_update",
    )(pairs, live, row1, row2, col1, col2, trailing)


def per_device(
    panel_first, panel_second, diag_first, bridge, diag_second, trailing, trail_pairs, live_count
):
    whole_first = lax.all_gather(diag_first, "col", axis=0, tiled=True)
    whole_bridge = lax.all_gather(bridge, "col", axis=0, tiled=True)
    whole_second = lax.all_gather(diag_second, "col", axis=0, tiled=True)

    first_h, first_l = inverse_factor(whole_first)
    lower_first = (dot_nt(panel_first[0], first_h) + dot_nt(panel_first[0], first_l)).astype(BF16)
    row_first = lax.all_gather(lower_first, "col", axis=0)
    col_first = lax.all_gather(lower_first, "row", axis=0)
    coupling = dot_nt(whole_bridge, first_h) + dot_nt(whole_bridge, first_l)
    c_high, c_low = split_outside(coupling)
    cross = dot_nt(c_high, c_low)
    shifted = whole_second.astype(F32) - (dot_nt(c_high, c_high) + cross + cross.T)
    second_h, second_l = inverse_factor(shifted)
    reduced = panel_second[0].astype(F32) - (dot_nt(lower_first, c_high) + dot_nt(lower_first, c_low))
    r_high, r_low = split_outside(reduced)
    lower_second = (
        dot_nt(r_high, second_h) + dot_nt(r_high, second_l) + dot_nt(r_low, second_h)
    ).astype(BF16)
    row_second = lax.all_gather(lower_second, "col", axis=0)
    col_second = lax.all_gather(lower_second, "row", axis=0)
    owned = trailing_update(
        trail_pairs[0], live_count, row_first, row_second, col_first, col_second, trailing[0]
    )
    return (lower_first[None], lower_second[None], owned[None])


def solution(mesh):
    return jax.shard_map(
        per_device,
        mesh=mesh,
        in_specs=(
            P(("row", "col"), None, None),
            P(("row", "col"), None, None),
            P("col", None),
            P("col", None),
            P("col", None),
            P(("row", "col"), None, None, None),
            P(("row", "col"), None, None),
            P(("row", "col")),
        ),
        out_specs=(
            P(("row", "col"), None, None),
            P(("row", "col"), None, None),
            P(("row", "col"), None, None, None),
        ),
        check_vma=False,
    )
```

time: 1170 us -> 366 us (0.31); the launches traced: 1150 us -> 360 us
  other arithmetic: 522 us -> 0 us
  matrix products: 212 us -> 28.1 us
  local copies, waits for them, and re-layouts: 132 us -> 11.3 us
  Pallas kernels: 0 us -> 105 us
  loops' own time: 103 us -> 0 us
  waiting for transfers between devices: 156 us -> 200 us
    another operation x66 -> x0, other arithmetic: 513 us -> none  [the longest x31 173 us: per_device(): factor_second = jnp.linalg.cholesky(shifted)]
    another operation x73 -> x0, matrix products: 124 us -> none  [the longest x45 77.9 us: right_solve(): jax.scipy.linalg.solve_triangular(lower_factor, block_rows.T, lower=True)]
    pallas_call x0 -> x3, Pallas kernels: none -> 105 us  [the longest x2 84.5 us: inverse_factor(): pl.pallas_call(factor_kernel, out_shape=[jax.ShapeDtypeStruct((size, size...]
    another operation x3 -> x0, loops' own time: 103 us -> none  [the longest x1 103 us: apply_owned(): return lax.fori_loop(first_slot, stop_slot, step_index, trailing)]
    dot_general x26 -> x11, matrix products: 88 us -> 28.1 us  [dot_nt(): lax.dot_general(left, right, (((1,), (1,)), ((), ())), preferred_element_...]
    another operation x67 -> x0, local copies, waits for them, and re-layouts: 51.2 us -> none  [the longest x51 46.1 us: right_solve(): jax.scipy.linalg.solve_triangular(lower_factor, block_rows.T, lower=True)]
    all_gather x5 -> x7, waiting for transfers between devices: 155 us -> 196 us  [the longest x1 46.7 us: per_device(): col_first = lax.all_gather(lower_first, 'row', axis=0)]
    dynamic_slice x48 -> x0, local copies, waits for them, and re-layouts: 37.8 us -> none  [the longest x24 23.4 us: step_index(): current = lax.dynamic_index_in_dim(carried, slot_index, 0, keepdims=False)]
  transfers between devices with their start and end apart: 5 -> 7, of which waited for: 3 -> 5; matrix products, arithmetic and copies ran while one was open for 32% -> 6% of each run, Pallas kernels for 0% -> 12%
where the time goes in v1:
time: 366 us; the launch traced here: 360 us
  waiting for transfers between devices  200 us (55%)
  Pallas kernels  105 us (29%)
  matrix products  28.1 us (8%)
  between operations  15 us (4%)
  local copies, waits for them, and re-layouts  11.3 us (3%)
    pallas_call x2, Pallas kernels, inverse_factor(): pl.pallas_call(factor_kernel, out_shape=[jax.ShapeDtypeStruct((size, size...  84.5 us
    all_gather x1, waiting for transfers between devices, per_device(): col_first = lax.all_gather(lower_first, 'row', axis=0)  46.7 us
    all_gather x1, waiting for transfers between devices, per_device(): col_second = lax.all_gather(lower_second, 'row', axis=0)  42.2 us
    all_gather x1, waiting for transfers between devices, per_device(): row_first = lax.all_gather(lower_first, 'col', axis=0)  39.2 us
    all_gather x1, waiting for transfers between devices, per_device(): row_second = lax.all_gather(lower_second, 'col', axis=0)  39.1 us
    all_gather x1, waiting for transfers between devices, per_device(): whole_first = lax.all_gather(diag_first, 'col', axis=0, tiled=True)  29 us
    dot_general x11, matrix products, dot_nt(): lax.dot_general(left, right, (((1,), (1,)), ((), ())), preferred_element_...  28.1 us
    pallas_call x1, Pallas kernels, trailing_update(): pl.pallas_call(trailing_kernel, out_shape=jax.ShapeDtypeStruct(trailing.s...  20.5 us
  transfers between devices with their start and end apart: 7, of which 5 were waited for; matrix products, arithmetic and copies ran while one was open for 6% of the time, Pallas kernels for 12%

profile of v1, /device:TPU:15, one launch (start us, length us, event | category | flops | bytes accessed | tf_op | source)
XLA Modules:
  0.0 359.7 jit_solution(11803057235294022706)
XLA Ops:
  7.2 0.0 copy-start
  7.2 0.0 all-gather.12.cloned.1.call-start
  7.2 0.7 all-gather.12.cloned.1.call-update
  7.9 0.0 all-gather.14.cloned.1.call-start
  8.0 0.7 all-gather.14.cloned.1.call-update
  8.7 0.0 all-gather.16.cloned.1.call-start
  8.7 0.7 all-gather.16.cloned.1.call-update
  9.4 0.0 all-gather.24.cloned.1.call-start
  9.4 29.0 %all-gather.12.cloned.1.call-done.a_ref = bf16[1024,1024]{1,0:T(8,128)(2,1)} async-done(((bf16[128,1024]{1,0:T(8,128)(2,1)}), bf16[1024,1024]{1,0:T(8,128)(2,1)}) %all-gather.12.cloned.1.call-update) | async-done | bytes 2097168 | tf_op jit(solution)/shard_map/all_gather | solution.py:197
  38.4 0.0 copy-start.5
  38.4 1.6 copy-done.5
  40.0 42.3 %inverse_factor.2 = (bf16[1024,1024]{1,0:T(8,128)(2,1)S(1)}, bf16[1024,1024]{1,0:T(8,128)(2,1)S(1)}) custom-call(bf16[1024,1024]{1,0:T(8,128)(2,1)S(1)} %copy-done.5), custom_call_target="tpu_custom_call" | custom-call | flops 60000002048 | bytes 8388608 | tf_op jit(solution)/shard_map/inverse_factor/pallas_call | solution.py:137
  82.3 0.0 copy-start.2
  82.3 1.4 copy-done.2
  83.7 0.0 all-gather.14.cloned.1.call-done
  83.7 0.0 copy-start.3
  83.7 0.0 copy-start.10
  83.7 4.1 %fusion.15 = f32[1024,1024]{1,0:T(8,128)S(1)} fusion(bf16[1024,1024]{1,0:T(8,128)(2,1)} %all-gather.14.cloned.1.call-done, bf16[1024,1024]{1,0:T(8,128)(2,1)S(1)} %get-tuple-element.7), kind=kOutput, calls=%fused_computation.22 | convolution fusion | flops 2147483648 | bytes 8388608 | tf_op jit(solution)/shard_map/dot_general | solution.py:43
  87.8 0.0 copy-done.3
  87.8 0.0 copy-done.10
  87.8 2.4 convolution_add_fusion
  90.2 0.0 copy-start.6
  90.2 1.9 copy-done.6
  92.1 4.4 %fusion.6 = f32[1024,1024]{1,0:T(8,128)} fusion(f32[1024,1024]{1,0:T(8,128)S(1)} %convolution_add_fusion), kind=kOutput, calls=%fused_computation.16 | convolution fusion | flops 2152726528 | bytes 8388608 | tf_op jit(solution)/shard_map/dot_general | solution.py:43
  96.5 5.5 %copy.11 = f32[1024,1024]{0,1:T(8,128)} copy(f32[1024,1024]{1,0:T(8,128)} %fusion.6) | data formatting | bytes 8388608 | tf_op jit(solution)/shard_map/dot_general | solution.py:43
  102.0 0.0 copy-done
  102.0 0.0 copy-start.4
  102.0 0.7 fusion.11
  102.8 0.8 copy-done.4
  103.6 0.7 fusion.3
  104.4 0.0 copy-start.8
  104.4 3.1 fusion.14
  107.5 0.0 all-gather.16.cloned.1.call-done
  107.5 8.8 %fusion.1.a_ref = f32[1024,1024]{1,0:T(8,128)S(1)} fusion(f32[1024,1024]{0,1:T(8,128)} %copy.11, f32[1024,1024]{1,0:T(8,128)} %fusion.6, bf16[1024,1024]{1,0:T(8,128)(2,1)} %all-gather.16.cloned.1.call-done, f32[1024,1024]{1,0:T(8,128)} %copy-done.6), kind=kOutput, calls=%fused_computation.4 | convolution fusion | flops 2153775104 | bytes 18874368 | tf_op jit(solution)/shard_map/dot_general | solution.py:43
  116.4 0.0 copy-start.7
  116.4 0.0 copy-start.9
  116.4 42.2 %inverse_factor.3 = (bf16[1024,1024]{1,0:T(8,128)(2,1)S(1)}, bf16[1024,1024]{1,0:T(8,128)(2,1)S(1)}) custom-call(f32[1024,1024]{1,0:T(8,128)S(1)} %fusion.1.a_ref), custom_call_target="tpu_custom_call" | custom-call | flops 60000002048 | bytes 8388608 | tf_op jit(solution)/shard_map/inverse_factor/pallas_call | solution.py:137
  158.7 0.0 copy-done.8
  158.7 0.0 copy-done.7
  158.7 0.0 copy-done.9
  158.7 0.8 fusion.2
  159.5 0.7 fusion.13
  160.2 0.8 convolution_add_fusion.2
  161.0 1.6 fusion.4
  162.5 0.0 all-gather.24.cloned.1.call-update
  162.5 0.0 all-gather.22.cloned.1.call-start
  162.6 0.5 all-gather.22.cloned.1.call-update
  163.1 0.0 all-gather.20.cloned.1.call-start
  163.2 0.5 all-gather.20.cloned.1.call-update
  163.7 0.0 all-gather.18.cloned.1.call-start
  163.8 0.7 all-gather.18.cloned.1.call-update
  165.1 42.2 %all-gather.24.cloned.1.call-done = bf16[1024,1024]{1,0:T(8,128)(2,1)} async-done(((bf16[256,1024]{1,0:T(8,128)(2,1)}), bf16[1024,1024]{1,0:T(8,128)(2,1)}) %all-gather.24.cloned.1.call-update) | async-done | bytes 2097168 | tf_op jit(solution)/shard_map/all_gather | solution.py:216
  207.3 46.7 %all-gather.22.cloned.1.call-done = bf16[1024,1024]{1,0:T(8,128)(2,1)} async-done(((bf16[256,1024]{1,0:T(8,128)(2,1)}), bf16[1024,1024]{1,0:T(8,128)(2,1)}) %all-gather.22.cloned.1.call-update) | async-done | bytes 2097168 | tf_op jit(solution)/shard_map/all_gather | solution.py:204
  254.0 39.1 %all-gather.20.cloned.1.call-done = bf16[2048,1024]{1,0:T(8,128)(2,1)} async-done(((bf16[256,1024]{1,0:T(8,128)(2,1)}), bf16[2048,1024]{1,0:T(8,128)(2,1)}) %all-gather.20.cloned.1.call-update) | async-done | bytes 4194320 | tf_op jit(solution)/shard_map/all_gather | solution.py:215
  293.1 39.2 %all-gather.18.cloned.1.call-done = bf16[2048,1024]{1,0:T(8,128)(2,1)} async-done(((bf16[256,1024]{1,0:T(8,128)(2,1)}), bf16[2048,1024]{1,0:T(8,128)(2,1)}) %all-gather.18.cloned.1.call-update) | async-done | bytes 4194320 | tf_op jit(solution)/shard_map/all_gather | solution.py:203
  332.3 0.0 copy-start.1
  332.3 20.5 %trailing_update.1 = f32[24,256,256]{2,1,0:T(8,128)} custom-call(s32[2,24]{1,0:T(2,128)} %bitcast.40, s32[1]{0:T(128)S(6)} %copy.12.live_ref, bf16[8,256,1024]{2,1,0:T(8,128)(2,1)} %bitcast.37, bf16[8,256,1024]{2,1,0:T(8,128)(2,1)} %bitcast.36, bf16[4,256,1024]{2,1,0:T(8,128)(2,1)} %bitcast.39, bf16[4,256,1024]{2,1,0:T(8,128)(2,1)} %bitcast.38, ...), custom_call_target="tpu_custom_call" | custom-call | flops 6442450944 | bytes 31457280 | tf_op jit(solution)/shard_map/trailing_update/pallas_call | solution.py:177
  352.9 0.0 copy-done.1
Async XLA Ops:
  7.2 94.9 %copy-start = (bf16[1,256,1024]{2,1,0:T(8,128)(2,1)S(1)}, bf16[1,256,1024]{2,1,0:T(8,128)(2,1)}, u32[]{:S(2)}) copy-start(bf16[1,256,1024]{2,1,0:T(8,128)(2,1)} %param.8) | copy-start | bytes 1572868
  7.2 31.3 %all-gather.12.cloned.1.call-start = ((), (), s32[]{:S(2)}) async-start(), calls=%async_computation | async-start | bytes 2359296 | tf_op jit(solution)/shard_map/all_gather | solution.py:197
  7.9 75.8 %all-gather.14.cloned.1.call-start = ((), (), s32[]{:S(2)}) async-start(), calls=%async_computation.1 | async-start | bytes 2359296 | tf_op jit(solution)/shard_map/all_gather | solution.py:198
  8.7 98.9 %all-gather.16.cloned.1.call-start = ((), (), s32[]{:S(2)}) async-start(), calls=%async_computation.2 | async-start | bytes 2359296 | tf_op jit(solution)/shard_map/all_gather | solution.py:199
  9.4 197.9 %all-gather.24.cloned.1.call-start = ((), (), s32[]{:S(2)}) async-start(), calls=%async_computation.6 | async-start | bytes 2621440 | tf_op jit(solution)/shard_map/all_gather | solution.py:216
  38.4 1.6 copy-start.5
  82.3 1.4 copy-start.2
  83.7 4.1 %copy-start.3 = (bf16[1024,1024]{1,0:T(8,128)(2,1)S(1)}, bf16[1024,1024]{1,0:T(8,128)(2,1)}, u32[]{:S(2)}) copy-start(bf16[1024,1024]{1,0:T(8,128)(2,1)} %copy-done.2) | copy-start | bytes 6291460
  83.7 4.1 %copy-start.10 = (bf16[1024,1024]{1,0:T(8,128)(2,1)S(1)}, bf16[1024,1024]{1,0:T(8,128)(2,1)}, u32[]{:S(2)}) copy-start(bf16[1024,1024]{1,0:T(8,128)(2,1)} %all-gather.14.cloned.1.call-done) | copy-start | bytes 6291460
  90.2 2.0 copy-start.6
  102.0 1.6 copy-start.4
  104.4 54.3 %copy-start.8 = (bf16[256,1024]{1,0:T(8,128)(2,1)}, bf16[256,1024]{1,0:T(8,128)(2,1)S(1)}, u32[]{:S(2)}) copy-start(bf16[256,1024]{1,0:T(8,128)(2,1)S(1)} %fusion.3) | copy-start | bytes 1572868
  116.4 42.3 %copy-start.7 = (f32[1024,1024]{1,0:T(8,128)S(1)}, f32[1024,1024]{1,0:T(8,128)}, u32[]{:S(2)}) copy-start(f32[1024,1024]{1,0:T(8,128)} %copy-done.6) | copy-start | bytes 12582916
  116.4 42.3 %copy-start.9 = (bf16[1,256,1024]{2,1,0:T(8,128)(2,1)S(1)}, bf16[1,256,1024]{2,1,0:T(8,128)(2,1)}, u32[]{:S(2)}) copy-start(bf16[1,256,1024]{2,1,0:T(8,128)(2,1)} %param.9) | copy-start | bytes 1572868
  162.5 91.4 %all-gather.22.cloned.1.call-start = ((), (), s32[]{:S(2)}) async-start(), calls=%async_computation.5 | async-start | bytes 2621440 | tf_op jit(solution)/shard_map/all_gather | solution.py:204
  163.1 130.0 %all-gather.20.cloned.1.call-start = ((), (), s32[]{:S(2)}) async-start(), calls=%async_computation.4 | async-start | bytes 4718592 | tf_op jit(solution)/shard_map/all_gather | solution.py:215
  163.7 168.6 %all-gather.18.cloned.1.call-start = ((), (), s32[]{:S(2)}) async-start(), calls=%async_computation.3 | async-start | bytes 4718592 | tf_op jit(solution)/shard_map/all_gather | solution.py:203
  332.3 20.5 %copy-start.1 = (bf16[1,256,1024]{2,1,0:T(8,128)(2,1)S(1)}, bf16[1,256,1024]{2,1,0:T(8,128)(2,1)}, u32[]{:S(2)}) copy-start(bf16[1,256,1024]{2,1,0:T(8,128)(2,1)} %param.8) | copy-start | bytes 1572868
Sparse Core Ops, SparseCore 0:
  9.9 28.4 all-gather.11
  40.3 27.9 all-gather.13
  70.2 27.9 all-gather.15
  162.7 44.5 all-gather.23
  209.3 44.6 all-gather.21
  256.3 36.7 all-gather.19
  295.6 36.7 all-gather.17

commit v2 on v1

--- a/solution.py
+++ b/solution.py
@@ -10,13 +10,9 @@
 BLOCK = 128
 MICRO = 16
 HALF = 8
+CHUNK = 256
 F32 = jnp.float32
 BF16 = jnp.bfloat16
-
-
-def split_outside(x):
-    high = lax.reduce_precision(x, 8, 7)
-    return high.astype(BF16), (x - high).astype(BF16)
 
 
 def split2(x):
@@ -97,10 +93,9 @@
     return jnp.concatenate(done, axis=0)
 
 
-def factor_kernel(a_ref, high_ref, low_ref, grid_ref, terms_ref, flipped_ref):
-    size = a_ref.shape[0]
+def run_factor(high_ref, low_ref, grid_ref, terms_ref, flipped_ref):
+    size = grid_ref.shape[0]
     blocks = size // BLOCK
-    grid_ref[...] = a_ref[...].astype(F32)
 
     @pl.loop(0, blocks)
     def _(k):
@@ -131,98 +126,214 @@
         low_ref[here, :] = final_l
 
 
-def inverse_factor(block):
-    size = block.shape[0]
+def first_kernel(a_ref, *refs):
+    high_ref, low_ref, grid_ref, terms_ref, flipped_ref = refs[-5:]
+    grid_ref[...] = a_ref[...].astype(F32)
+    run_factor(high_ref, low_ref, grid_ref, terms_ref, flipped_ref)
+
+
+def second_kernel(bridge_ref, fh_ref, fl_ref, d_ref, *refs):
+    ch_ref, cl_ref, high_ref, low_ref, grid_ref, terms_ref, flipped_ref = refs[-7:]
+    size = d_ref.shape[0]
+
+    @pl.loop(0, size // CHUNK)
+    def _(i):
+        rows = pl.ds(pl.multiple_of(i * CHUNK, CHUNK), CHUNK)
+        for first in range(0, size, CHUNK):
+            last = first + CHUNK
+            part = bridge_ref[rows, :last]
+            value = dot_nt(part, fh_ref[first:last, :last]) + dot_nt(part, fl_ref[first:last, :last])
+            ch_ref[rows, first:last], cl_ref[rows, first:last] = split2(value)
+
+    @pl.loop(0, size // CHUNK)
+    def _(i):
+        rows = pl.ds(pl.multiple_of(i * CHUNK, CHUNK), CHUNK)
+        part_h, part_l = ch_ref[rows, :], cl_ref[rows, :]
+        for first in range(0, size, CHUNK):
+            last = first + CHUNK
+            other_h, other_l = ch_ref[first:last, :], cl_ref[first:last, :]
+            product = dot_nt(part_h, other_h) + (dot_nt(part_h, other_l) + dot_nt(part_l, other_h))
+            grid_ref[rows, first:last] = d_ref[rows, first:last].astype(F32) - product
+
+    run_factor(high_ref, low_ref, grid_ref, terms_ref, flipped_ref)
+
+
+def factor_call(kernel, outs, name, operands, arrived):
+    size = operands[0].shape[0]
     whole = pl.BlockSpec(memory_space=pltpu.VMEM)
     return pl.pallas_call(
-        factor_kernel,
-        out_shape=[jax.ShapeDtypeStruct((size, size), BF16)] * 2,
-        in_specs=[whole],
-        out_specs=[whole, whole],
+        kernel,
+        out_shape=[jax.ShapeDtypeStruct((size, size), BF16)] * outs,
+        in_specs=[whole] * len(operands) + [pl.BlockSpec(memory_space=pl.ANY)] * len(arrived),
+        out_specs=[whole] * outs,
         scratch_shapes=[
             pltpu.VMEM((size, size), F32),
             pltpu.VMEM((3 * BLOCK, size), BF16),
             pltpu.VMEM((3 * BLOCK, size), BF16),
         ],
-        compiler_params=pltpu.CompilerParams(vmem_limit_bytes=40 * 2**20),
+        compiler_params=pltpu.CompilerParams(vmem_limit_bytes=48 * 2**20),
         cost_estimate=pl.CostEstimate(flops=60 * 10**9, bytes_accessed=8 * 2**20, transcendentals=0),
-        name="inverse_factor",
-    )(block)
-
-
-def trailing_kernel(pairs_ref, live_ref, row1_ref, row2_ref, col1_ref, col2_ref, in_ref, out_ref):
+        name=name,
+    )(*operands, *arrived)
+
+
+def solve_kernel(tile_ref, high_ref, low_ref, second_ref, *refs):
+    lower_ref, again_ref = refs[-2:]
+    panel = tile_ref.shape[1]
+    for first in range(0, panel, CHUNK):
+        last = first + CHUNK
+        part = tile_ref[:, :last]
+        value = dot_nt(part, high_ref[first:last, :last]) + dot_nt(part, low_ref[first:last, :last])
+        lower_ref[:, first:last] = value.astype(BF16)
+    again_ref[...] = second_ref[...]
+
+
+def first_solve(tile, high, low, second, arrived):
+    whole = pl.BlockSpec(memory_space=pltpu.VMEM)
+    return pl.pallas_call(
+        solve_kernel,
+        out_shape=[jax.ShapeDtypeStruct(tile.shape, BF16)] * 2,
+        in_specs=[whole] * 4 + [pl.BlockSpec(memory_space=pl.ANY)] * len(arrived),
+        out_specs=[whole] * 2,
+        compiler_params=pltpu.CompilerParams(vmem_limit_bytes=32 * 2**20),
+        name="first_solve",
+    )(tile, high, low, second, *arrived)
+
+
+def finish_kernel(tiles, n_col, pairs_ref, live_ref, origin_ref, ch_ref, cl_ref, wh_ref, wl_ref, *refs):
+    gathered, seconds, firsts = refs[0], refs[1 : 1 + tiles], refs[1 + tiles : 1 + 2 * tiles - n_col]
+    in_ref, lower_ref, out_ref, x_ref, y_ref, rh_ref, rl_ref, sems = refs[-8:]
     slot = pl.program_id(0)
+    panel = x_ref.shape[-1]
+
+    @pl.when(slot == 0)
+    def _():
+        copies = []
+        for t in range(tiles):
+            source = gathered.at[origin_ref[t]] if t < n_col else firsts[t - n_col]
+            copies.append(pltpu.make_async_copy(source, x_ref.at[t], sems.at[0, t]))
+            copies.append(pltpu.make_async_copy(seconds[t], y_ref.at[t], sems.at[1, t]))
+        for copy in copies:
+            copy.start()
+        for copy in copies:
+            copy.wait()
+
+        @pl.loop(0, tiles)
+        def _(t):
+            lower = x_ref[t]
+            for first in range(0, panel, CHUNK):
+                part = slice(first, first + CHUNK)
+                reduced = y_ref[t, :, part].astype(F32) - (
+                    dot_nt(lower, ch_ref[part, :]) + dot_nt(lower, cl_ref[part, :])
+                )
+                rh_ref[:, part], rl_ref[:, part] = split2(reduced)
+            for first in range(0, panel, CHUNK):
+                last = first + CHUNK
+                high, low = rh_ref[:, :last], rl_ref[:, :last]
+                w_high, w_low = wh_ref[first:last, :last], wl_ref[first:last, :last]
+                value = dot_nt(high, w_high) + (dot_nt(high, w_low) + dot_nt(low, w_high))
+                y_ref[t, :, first:last] = value.astype(BF16)
+
+        lower_ref[...] = y_ref[0]
 
     @pl.when(slot < live_ref[0])
     def _():
         a = pairs_ref[0, slot]
         b = pairs_ref[1, slot]
-        out_ref[0] = (
-            in_ref[0] - dot_nt(row1_ref[a], col1_ref[b]) - dot_nt(row2_ref[a], col2_ref[b])
-        )
+        out_ref[0] = in_ref[0] - (dot_nt(x_ref[a], x_ref[b]) + dot_nt(y_ref[a], y_ref[b]))
 
     @pl.when(slot >= live_ref[0])
     def _():
         out_ref[0] = in_ref[0]
 
 
-def trailing_update(pairs, live, row1, row2, col1, col2, trailing):
+def finish(pairs, live, origin, couplings, inverses, gathered, seconds, firsts, trailing):
     slots, tile, _ = trailing.shape
-    panel = row1.shape[-1]
-
-    def whole(array):
-        return pl.BlockSpec(array.shape, lambda s, *_: (0, 0, 0), pipeline_mode=pl.Buffered(1))
-
+    n_col, _, panel = gathered.shape
+    tiles = len(seconds)
+    fixed = pl.BlockSpec((panel, panel), lambda s, *_: (0, 0), pipeline_mode=pl.Buffered(1))
     one = pl.BlockSpec((1, tile, tile), lambda s, *_: (s, 0, 0))
     return pl.pallas_call(
-        trailing_kernel,
-        out_shape=jax.ShapeDtypeStruct(trailing.shape, F32),
+        functools.partial(finish_kernel, tiles, n_col),
+        out_shape=[
+            jax.ShapeDtypeStruct((tile, panel), BF16),
+            jax.ShapeDtypeStruct(trailing.shape, F32),
+        ],
         grid_spec=pltpu.PrefetchScalarGridSpec(
-            num_scalar_prefetch=2,
+            num_scalar_prefetch=3,
             grid=(slots,),
-            in_specs=[whole(row1), whole(row2), whole(col1), whole(col2), one],
-            out_specs=one,
+            in_specs=[fixed] * 4 + [pl.BlockSpec(memory_space=pl.ANY)] * (1 + 2 * tiles - n_col) + [one],
+            out_specs=[pl.BlockSpec((tile, panel), lambda s, *_: (0, 0)), one],
+            scratch_shapes=[
+                pltpu.VMEM((tiles, tile, panel), BF16),
+                pltpu.VMEM((tiles, tile, panel), BF16),
+                pltpu.VMEM((tile, panel), BF16),
+                pltpu.VMEM((tile, panel), BF16),
+                pltpu.SemaphoreType.DMA((2, tiles)),
+            ],
         ),
         compiler_params=pltpu.CompilerParams(vmem_limit_bytes=56 * 2**20),
         cost_estimate=pl.CostEstimate(
-            flops=4 * slots * tile * tile * panel, bytes_accessed=30 * 2**20, transcendentals=0
+            flops=4 * slots * tile * tile * panel + 10 * tiles * tile * panel * panel,
+            bytes_accessed=30 * 2**20,
+            transcendentals=0,
         ),
-        name="trailing_update",
-    )(pairs, live, row1, row2, col1, col2, trailing)
+        name="solve_and_update",
+    )(pairs, live, origin, *couplings, *inverses, gathered, *seconds, *firsts, trailing)
+
+
+def shifted_copies(array, name, count, start=1, stop=None):
+    return [
+        lax.ppermute(array, name, [(i, (i + s) % count) for i in range(count)])
+        for s in range(start, count if stop is None else stop)
+    ]
 
 
 def per_device(
-    panel_first, panel_second, diag_first, bridge, diag_second, trailing, trail_pairs, live_count
+    n_row, n_col,
+    panel_first, panel_second, diag_first, bridge, diag_second, trailing, trail_pairs, live_count,
 ):
     whole_first = lax.all_gather(diag_first, "col", axis=0, tiled=True)
     whole_bridge = lax.all_gather(bridge, "col", axis=0, tiled=True)
     whole_second = lax.all_gather(diag_second, "col", axis=0, tiled=True)
-
-    first_h, first_l = inverse_factor(whole_first)
-    lower_first = (dot_nt(panel_first[0], first_h) + dot_nt(panel_first[0], first_l)).astype(BF16)
-    row_first = lax.all_gather(lower_first, "col", axis=0)
-    col_first = lax.all_gather(lower_first, "row", axis=0)
-    coupling = dot_nt(whole_bridge, first_h) + dot_nt(whole_bridge, first_l)
-    c_high, c_low = split_outside(coupling)
-    cross = dot_nt(c_high, c_low)
-    shifted = whole_second.astype(F32) - (dot_nt(c_high, c_high) + cross + cross.T)
-    second_h, second_l = inverse_factor(shifted)
-    reduced = panel_second[0].astype(F32) - (dot_nt(lower_first, c_high) + dot_nt(lower_first, c_low))
-    r_high, r_low = split_outside(reduced)
-    lower_second = (
-        dot_nt(r_high, second_h) + dot_nt(r_high, second_l) + dot_nt(r_low, second_h)
-    ).astype(BF16)
-    row_second = lax.all_gather(lower_second, "col", axis=0)
-    col_second = lax.all_gather(lower_second, "row", axis=0)
-    owned = trailing_update(
-        trail_pairs[0], live_count, row_first, row_second, col_first, col_second, trailing[0]
+    one, two = 1 + 3 * n_col // 8, 1 + 5 * n_col // 8
+    early = shifted_copies(panel_second[0], "col", n_col, 1, one)
+    middle = shifted_copies(panel_second[0], "col", n_col, one, two)
+    second_row = shifted_copies(panel_second[0], "row", n_row)
+
+    r, c = lax.axis_index("row"), lax.axis_index("col")
+    up = (r - trail_pairs[0, 1] + n_row) % n_row
+    pairs = jnp.stack(
+        [(c - trail_pairs[0, 0] + n_col) % n_col, jnp.where(up == 0, 0, n_col - 1 + up)]
+    )
+
+    first_h, first_l = factor_call(first_kernel, 2, "first_factor", [whole_first], early)
+    lower_first, second_again = first_solve(
+        panel_first[0], first_h, first_l, panel_second[0], second_row + middle
+    )
+    late = shifted_copies(second_again, "col", n_col, two)
+    first_col = lax.all_gather(lower_first, "col", axis=0)
+    first_row = shifted_copies(lower_first, "row", n_row)
+    c_high, c_low, second_h, second_l = factor_call(
+        second_kernel, 4, "second_factor", [whole_bridge, first_h, first_l, whole_second], []
+    )
+    lower_second, owned = finish(
+        pairs,
+        live_count,
+        (c - jnp.arange(n_col, dtype=jnp.int32) + n_col) % n_col,
+        (c_high, c_low),
+        (second_h, second_l),
+        first_col,
+        [panel_second[0]] + early + middle + late + second_row,
+        first_row,
+        trailing[0],
     )
     return (lower_first[None], lower_second[None], owned[None])
 
 
 def solution(mesh):
     return jax.shard_map(
-        per_device,
+        functools.partial(per_device, mesh.shape["row"], mesh.shape["col"]),
         mesh=mesh,
         in_specs=(
             P(("row", "col"), None, None),

time: 366 us -> 257 us (0.70)
  the two profiles are of different devices: /device:TPU:15 before, /device:TPU:7 now
where the time goes in v2:
time: 257 us; the launch traced here: 256 us
  Pallas kernels  154 us (60%)
  waiting for transfers between devices  57.1 us (22%)
  starting transfers between devices  18.8 us (7%)
  between operations  14.6 us (6%)
  local copies, waits for them, and re-layouts  10.5 us (4%)
    pallas_call x2, Pallas kernels, factor_call(): pl.pallas_call(kernel, out_shape=[jax.ShapeDtypeStruct((size, size), BF16...  102 us
    pallas_call x1, Pallas kernels, finish(): pl.pallas_call(functools.partial(finish_kernel, tiles, n_col), out_shape=...  49.7 us
    all_gather x1, waiting for transfers between devices, per_device(): whole_second = lax.all_gather(diag_second, 'col', axis=0, tiled=True)  19.9 us
    ppermute x13, starting transfers between devices, shifted_copies(): lax.ppermute(array, name, [(i, (i + s) % count) for i in range(count)])  18.6 us
    ppermute x13, waiting for transfers between devices, shifted_copies(): lax.ppermute(array, name, [(i, (i + s) % count) for i in range(count)])  17.9 us
    all_gather x1, waiting for transfers between devices, per_device(): whole_first = lax.all_gather(diag_first, 'col', axis=0, tiled=True)  17.9 us
    unnamed x38, local copies, waits for them, and re-layouts  10.5 us
  transfers between devices with their start and end apart: 17, of which 4 were waited for; matrix products, arithmetic and copies ran while one was open for 0% of the time, Pallas kernels for 41%

profile of v2, /device:TPU:7, one launch (start us, length us, event | category | flops | bytes accessed | tf_op | source)
XLA Modules:
  0.0 255.9 jit_solution(16150893539422951077)
XLA Ops:
  7.2 0.0 all-gather.6.cloned.1.call-start
  7.2 0.7 all-gather.6.cloned.1.call-update
  7.9 0.0 all-gather.8.cloned.1.call-start
  7.9 0.7 all-gather.8.cloned.1.call-update
  8.6 0.0 all-gather.10.cloned.1.call-start
  8.7 0.8 collective-permute-start.2
  9.5 1.2 collective-permute-start.1
  10.7 1.2 collective-permute-start
  11.9 0.0 collective-permute-start.7
  11.9 0.7 collective-permute-start.6
  12.6 0.0 all-gather.10.cloned.1.call-update
  12.7 0.0 all-gather.12.cloned.1.call-start
  12.7 13.2 %collective-permute-done.2.refs_2_.refs_4_ = bf16[256,1024]{1,0:T(8,128)(2,1)S(1)} collective-permute-done((bf16[256,1024]{1,0:T(8,128)(2,1)}, bf16[256,1024]{1,0:T(8,128)(2,1)S(1)}, u32[]{:S(2)}, u32[]{:S(2)}) %collective-permute-start.2) | collective-permute-done | bytes 524320 | tf_op jit(solution)/shard_map/ppermute | solution.py:287
  26.0 0.8 copy-done.4
  26.8 3.5 %collective-permute-start.5 = (bf16[256,1024]{1,0:T(8,128)(2,1)}, bf16[256,1024]{1,0:T(8,128)(2,1)}, u32[]{:S(2)}, u32[]{:S(2)}) collective-permute-start(bf16[256,1024]{1,0:T(8,128)(2,1)} %bitcast.19), channel_id=1, source_target_pairs={{0,24},{8,0},{16,8},{24,16},{1,25},{9,1},{17,9},{25,17},{2,26},{10... | collective-permute-start | bytes 1572872 | tf_op jit(solution)/shard_map/ppermute | solution.py:287
  30.3 0.0 collective-permute-done.1.refs_1_.refs_3_
  30.3 0.8 copy-done.6
  31.1 0.0 collective-permute-start.4
  31.1 4.7 %collective-permute-done.refs_0_.refs_2_ = bf16[256,1024]{1,0:T(8,128)(2,1)S(1)} collective-permute-done((bf16[256,1024]{1,0:T(8,128)(2,1)}, bf16[256,1024]{1,0:T(8,128)(2,1)S(1)}, u32[]{:S(2)}, u32[]{:S(2)}) %collective-permute-start) | collective-permute-done | bytes 524320 | tf_op jit(solution)/shard_map/ppermute | solution.py:287
  35.8 0.8 copy-done.8
  36.6 1.3 collective-permute-start.3
  37.9 17.9 %all-gather.6.cloned.1.call-done.a_ref = bf16[1024,1024]{1,0:T(8,128)(2,1)} async-done(((bf16[128,1024]{1,0:T(8,128)(2,1)}), bf16[1024,1024]{1,0:T(8,128)(2,1)}) %all-gather.6.cloned.1.call-update) | async-done | bytes 2097168 | tf_op jit(solution)/shard_map/all_gather | solution.py:296
  55.7 1.0 copy-done.5
  56.8 1.0 copy-done.7
  57.8 1.0 copy-done.9
  58.9 43.8 %first_factor.1 = (bf16[1024,1024]{1,0:T(8,128)(2,1)S(1)}, bf16[1024,1024]{1,0:T(8,128)(2,1)S(1)}) custom-call(bf16[1024,1024]{1,0:T(8,128)(2,1)} %all-gather.6.cloned.1.call-done.a_ref, bf16[256,1024]{1,0:T(8,128)(2,1)S(1)} %copy-done.9, bf16[256,1024]{1,0:T(8,128)(2,1)S(1)} %copy-done.7, bf16[256,1024]{1,0:T(8,128)(2,1)S(1)} %copy-done.5), custom_call_target="tpu_custom_call" | custom-call | flops 60000002048 | bytes 8388608 | tf_op jit(solution)/shard_map/first_factor/pallas_call | solution.py:164
  102.7 0.0 copy-start
  102.7 0.0 collective-permute-done.7.refs_4_.refs_6_
  102.7 0.0 collective-permute-done.6.refs_3_.refs_5_
  102.7 0.0 collective-permute-done.5.refs_2_.refs_11_
  102.7 0.0 collective-permute-done.4.refs_1_.refs_10_
  102.8 0.0 collective-permute-done.3.refs_0_.refs_9_
  102.8 0.0 copy-done.2
  102.8 0.0 copy-done.3
  102.8 0.0 copy-start.13
  102.8 2.1 first_solve.1
  104.9 0.0 copy-done.1
  104.9 0.8 copy-done.10
  105.7 0.0 all-gather.12.cloned.1.call-update
  106.3 0.6 and_select_fusion.origin_ref
  106.9 0.0 copy-done.13
  106.9 0.5 pad_add_fusion.pairs_ref
  107.5 0.3 collective-permute-start.9
  107.8 5.8 %collective-permute-start.8 = (bf16[256,1024]{1,0:T(8,128)(2,1)}, bf16[256,1024]{1,0:T(8,128)(2,1)S(1)}, u32[]{:S(2)}, u32[]{:S(2)}) collective-permute-start(bf16[256,1024]{1,0:T(8,128)(2,1)} %copy-done.10), channel_id=1, source_target_pairs={{0,6},{1,7},{2,0},{3,1},{4,2},{5,3},{6,4},{7,5},{8,14},{9,15},{10,... | collective-permute-start | bytes 1572872 | tf_op jit(solution)/shard_map/ppermute | solution.py:287
  113.5 3.3 %collective-permute-start.12 = (bf16[256,1024]{1,0:T(8,128)(2,1)}, bf16[256,1024]{1,0:T(8,128)(2,1)S(1)}, u32[]{:S(2)}, u32[]{:S(2)}) collective-permute-start(bf16[256,1024]{1,0:T(8,128)(2,1)} %get-tuple-element.15), channel_id=1, source_target_pairs={{0,24},{8,0},{16,8},{24,16},{1,25},{9,1},{17,9},{25,17},{2,26},{10... | collective-permute-start | bytes 1572872 | tf_op jit(solution)/shard_map/ppermute | solution.py:287
  116.8 0.0 collective-permute-start.11
  116.8 0.5 collective-permute-start.10
  117.3 19.9 %all-gather.10.cloned.1.call-done.d_ref = bf16[1024,1024]{1,0:T(8,128)(2,1)} async-done(((bf16[128,1024]{1,0:T(8,128)(2,1)}), bf16[1024,1024]{1,0:T(8,128)(2,1)}) %all-gather.10.cloned.1.call-update) | async-done | bytes 2097168 | tf_op jit(solution)/shard_map/all_gather | solution.py:298
  137.2 58.3 %second_factor.1 = (bf16[1024,1024]{1,0:T(8,128)(2,1)S(1)}, bf16[1024,1024]{1,0:T(8,128)(2,1)S(1)}, bf16[1024,1024]{1,0:T(8,128)(2,1)}, bf16[1024,1024]{1,0:T(8,128)(2,1)}) custom-call(bf16[1024,1024]{1,0:T(8,128)(2,1)} %all-gather.8.cloned.1.call-done.bridge_ref, bf16[1024,1024]{1,0:T(8,128)(2,1)} %copy-done, bf16[1024,1024]{1,0:T(8,128)(2,1)} %copy-done.1, ...), custom_call_target="tpu_custom_call" | custom-call | flops 60000002048 | bytes 8388608 | tf_op jit(solution)/shard_map/second_factor/pallas_call | solution.py:164
  195.5 1.3 copy-done.11
  196.8 1.4 copy-done.12
  198.2 0.0 collective-permute-done.9.refs_8_
  198.2 0.0 collective-permute-done.8.refs_7_
  198.2 0.0 collective-permute-done.12.refs_14_
  198.2 0.0 copy-start.16
  198.2 0.0 collective-permute-done.11.refs_13_
  198.3 0.0 collective-permute-done.10.refs_12_
  198.3 0.0 all-gather.12.cloned.1.call-done
  198.3 0.7 copy-done.14
  199.0 0.2 copy-done.15
  199.2 0.2 copy-done.16
  199.4 0.1 copy-done.17
  199.5 0.2 copy-done.18
  199.6 49.7 %solve_and_update.1 = (bf16[256,1024]{1,0:T(8,128)(2,1)}, f32[24,256,256]{2,1,0:T(8,128)}) custom-call(s32[2,24]{1,0:T(2,128)} %pad_add_fusion.pairs_ref, s32[1]{0:T(128)S(6)} %copy.11.live_ref, s32[8]{0:T(128)} %and_select_fusion.origin_ref, bf16[1024,1024]{1,0:T(8,128)(2,1)} %copy-done.11, bf16[1024,1024]{1,0:T(8,128)(2,1)} %copy-done.12, ...), custom_call_target="tpu_custom_call" | custom-call | flops 35970351104 | bytes 31457280 | tf_op jit(solution)/shard_map/solve_and_update/pallas_call | solution.py:256
  (19 shorter events, 0.0 us)
Async XLA Ops:
  7.2 48.6 %all-gather.6.cloned.1.call-start = ((), (), s32[]{:S(2)}) async-start(), calls=%async_computation | async-start | bytes 2359296 | tf_op jit(solution)/shard_map/all_gather | solution.py:296
  7.9 109.4 %all-gather.8.cloned.1.call-start = ((), (), s32[]{:S(2)}) async-start(), calls=%async_computation.1 | async-start | bytes 2359296 | tf_op jit(solution)/shard_map/all_gather | solution.py:297
  8.6 128.5 %all-gather.10.cloned.1.call-start = ((), (), s32[]{:S(2)}) async-start(), calls=%async_computation.2 | async-start | bytes 2359296 | tf_op jit(solution)/shard_map/all_gather | solution.py:298
  8.7 17.3 %collective-permute-start.2 = (bf16[256,1024]{1,0:T(8,128)(2,1)}, bf16[256,1024]{1,0:T(8,128)(2,1)S(1)}, u32[]{:S(2)}, u32[]{:S(2)}) collective-permute-start(bf16[256,1024]{1,0:T(8,128)(2,1)} %bitcast.14), channel_id=1, source_target_pairs={{0,3},{1,4},{2,5},{3,6},{4,7},{5,0},{6,1},{7,2},{8,11},{9,12},{10,... | collective-permute-start | bytes 1572872 | tf_op jit(solution)/shard_map/ppermute | solution.py:287
  9.5 20.8 %collective-permute-start.1 = (bf16[256,1024]{1,0:T(8,128)(2,1)}, bf16[256,1024]{1,0:T(8,128)(2,1)S(1)}, u32[]{:S(2)}, u32[]{:S(2)}) collective-permute-start(bf16[256,1024]{1,0:T(8,128)(2,1)} %bitcast.15), channel_id=1, source_target_pairs={{0,2},{1,3},{2,4},{3,5},{4,6},{5,7},{6,0},{7,1},{8,10},{9,11},{10,... | collective-permute-start | bytes 1572872 | tf_op jit(solution)/shard_map/ppermute | solution.py:287
  10.7 25.0 %collective-permute-start = (bf16[256,1024]{1,0:T(8,128)(2,1)}, bf16[256,1024]{1,0:T(8,128)(2,1)S(1)}, u32[]{:S(2)}, u32[]{:S(2)}) collective-permute-start(bf16[256,1024]{1,0:T(8,128)(2,1)} %bitcast.16), channel_id=1, source_target_pairs={{0,1},{1,2},{2,3},{3,4},{4,5},{5,6},{6,7},{7,0},{8,9},{9,10},{10,1... | collective-permute-start | bytes 1572872 | tf_op jit(solution)/shard_map/ppermute | solution.py:287
  11.9 90.8 %collective-permute-start.7 = (bf16[256,1024]{1,0:T(8,128)(2,1)}, bf16[256,1024]{1,0:T(8,128)(2,1)}, u32[]{:S(2)}, u32[]{:S(2)}) collective-permute-start(bf16[256,1024]{1,0:T(8,128)(2,1)} %bitcast.17), channel_id=1, source_target_pairs={{0,5},{1,6},{2,7},{3,0},{4,1},{5,2},{6,3},{7,4},{8,13},{9,14},{10,... | collective-permute-start | bytes 1572872 | tf_op jit(solution)/shard_map/ppermute | solution.py:287
  11.9 90.8 %collective-permute-start.6 = (bf16[256,1024]{1,0:T(8,128)(2,1)}, bf16[256,1024]{1,0:T(8,128)(2,1)}, u32[]{:S(2)}, u32[]{:S(2)}) collective-permute-start(bf16[256,1024]{1,0:T(8,128)(2,1)} %bitcast.18), channel_id=1, source_target_pairs={{0,4},{1,5},{2,6},{3,7},{4,0},{5,1},{6,2},{7,3},{8,12},{9,13},{10,... | collective-permute-start | bytes 1572872 | tf_op jit(solution)/shard_map/ppermute | solution.py:287
  12.7 90.1 %copy-start.2 = (bf16[1,256,1024]{2,1,0:T(8,128)(2,1)S(1)}, bf16[1,256,1024]{2,1,0:T(8,128)(2,1)}, u32[]{:S(2)}) copy-start(bf16[1,256,1024]{2,1,0:T(8,128)(2,1)} %param.8) | copy-start | bytes 1572868
  12.7 90.1 %copy-start.3 = (bf16[1,256,1024]{2,1,0:T(8,128)(2,1)S(1)}, bf16[1,256,1024]{2,1,0:T(8,128)(2,1)}, u32[]{:S(2)}) copy-start(bf16[1,256,1024]{2,1,0:T(8,128)(2,1)} %param.9) | copy-start | bytes 1572868
  12.7 185.6 %all-gather.12.cloned.1.call-start = ((), (), s32[]{:S(2)}) async-start(), calls=%async_computation.3 | async-start | bytes 4718592 | tf_op jit(solution)/shard_map/all_gather | solution.py:315
  26.0 0.8 copy-start.4
  26.8 76.0 %collective-permute-start.5 = (bf16[256,1024]{1,0:T(8,128)(2,1)}, bf16[256,1024]{1,0:T(8,128)(2,1)}, u32[]{:S(2)}, u32[]{:S(2)}) collective-permute-start(bf16[256,1024]{1,0:T(8,128)(2,1)} %bitcast.19), channel_id=1, source_target_pairs={{0,24},{8,0},{16,8},{24,16},{1,25},{9,1},{17,9},{25,17},{2,26},{10... | collective-permute-start | bytes 1572872 | tf_op jit(solution)/shard_map/ppermute | solution.py:287
  30.3 0.8 copy-start.6
  31.1 71.6 %collective-permute-start.4 = (bf16[256,1024]{1,0:T(8,128)(2,1)}, bf16[256,1024]{1,0:T(8,128)(2,1)}, u32[]{:S(2)}, u32[]{:S(2)}) collective-permute-start(bf16[256,1024]{1,0:T(8,128)(2,1)} %bitcast.20), channel_id=1, source_target_pairs={{0,16},{8,24},{16,0},{24,8},{1,17},{9,25},{17,1},{25,9},{2,18},{10... | collective-permute-start | bytes 1572872 | tf_op jit(solution)/shard_map/ppermute | solution.py:287
  35.8 0.8 copy-start.8
  36.6 66.2 %collective-permute-start.3 = (bf16[256,1024]{1,0:T(8,128)(2,1)}, bf16[256,1024]{1,0:T(8,128)(2,1)}, u32[]{:S(2)}, u32[]{:S(2)}) collective-permute-start(bf16[256,1024]{1,0:T(8,128)(2,1)} %bitcast.21), channel_id=1, source_target_pairs={{0,8},{8,16},{16,24},{24,0},{1,9},{9,17},{17,25},{25,1},{2,10},{10... | collective-permute-start | bytes 1572872 | tf_op jit(solution)/shard_map/ppermute | solution.py:287
  55.7 1.0 copy-start.5
  56.8 1.0 copy-start.7
  57.8 1.0 copy-start.9
  102.7 2.2 copy-start
  102.7 2.2 copy-start.1
  102.8 4.1 %copy-start.13 = (s32[1,2,24]{2,1,0:T(2,128)S(1)}, s32[1,2,24]{2,1,0:T(2,128)}, u32[]{:S(2)}) copy-start(s32[1,2,24]{2,1,0:T(2,128)} %param.14) | copy-start | bytes 580
  104.9 0.8 copy-start.10
  107.5 90.7 %collective-permute-start.9 = (bf16[256,1024]{1,0:T(8,128)(2,1)}, bf16[256,1024]{1,0:T(8,128)(2,1)S(1)}, u32[]{:S(2)}, u32[]{:S(2)}) collective-permute-start(bf16[256,1024]{1,0:T(8,128)(2,1)} %copy-done.10), channel_id=1, source_target_pairs={{0,7},{1,0},{2,1},{3,2},{4,3},{5,4},{6,5},{7,6},{8,15},{9,8},{10,9... | collective-permute-start | bytes 1572872 | tf_op jit(solution)/shard_map/ppermute | solution.py:287
  107.8 90.4 %collective-permute-start.8 = (bf16[256,1024]{1,0:T(8,128)(2,1)}, bf16[256,1024]{1,0:T(8,128)(2,1)S(1)}, u32[]{:S(2)}, u32[]{:S(2)}) collective-permute-start(bf16[256,1024]{1,0:T(8,128)(2,1)} %copy-done.10), channel_id=1, source_target_pairs={{0,6},{1,7},{2,0},{3,1},{4,2},{5,3},{6,4},{7,5},{8,14},{9,15},{10,... | collective-permute-start | bytes 1572872 | tf_op jit(solution)/shard_map/ppermute | solution.py:287
  113.5 84.7 %collective-permute-start.12 = (bf16[256,1024]{1,0:T(8,128)(2,1)}, bf16[256,1024]{1,0:T(8,128)(2,1)S(1)}, u32[]{:S(2)}, u32[]{:S(2)}) collective-permute-start(bf16[256,1024]{1,0:T(8,128)(2,1)} %get-tuple-element.15), channel_id=1, source_target_pairs={{0,24},{8,0},{16,8},{24,16},{1,25},{9,1},{17,9},{25,17},{2,26},{10... | collective-permute-start | bytes 1572872 | tf_op jit(solution)/shard_map/ppermute | solution.py:287
  116.8 81.4 %collective-permute-start.11 = (bf16[256,1024]{1,0:T(8,128)(2,1)}, bf16[256,1024]{1,0:T(8,128)(2,1)S(1)}, u32[]{:S(2)}, u32[]{:S(2)}) collective-permute-start(bf16[256,1024]{1,0:T(8,128)(2,1)} %get-tuple-element.15), channel_id=1, source_target_pairs={{0,16},{8,24},{16,0},{24,8},{1,17},{9,25},{17,1},{25,9},{2,18},{10... | collective-permute-start | bytes 1572872 | tf_op jit(solution)/shard_map/ppermute | solution.py:287
  116.8 81.4 %collective-permute-start.10 = (bf16[256,1024]{1,0:T(8,128)(2,1)}, bf16[256,1024]{1,0:T(8,128)(2,1)S(1)}, u32[]{:S(2)}, u32[]{:S(2)}) collective-permute-start(bf16[256,1024]{1,0:T(8,128)(2,1)} %get-tuple-element.15), channel_id=1, source_target_pairs={{0,8},{8,16},{16,24},{24,0},{1,9},{9,17},{17,25},{25,1},{2,10},{10... | collective-permute-start | bytes 1572872 | tf_op jit(solution)/shard_map/ppermute | solution.py:287
  195.5 1.3 copy-start.11
  196.8 1.4 copy-start.12
  198.2 0.8 copy-start.14
  198.2 1.0 copy-start.15
  198.2 1.1 copy-start.16
  198.2 1.2 copy-start.17
  198.3 1.4 copy-start.18
Sparse Core Ops, SparseCore 0:
  9.9 45.8 all-gather.5
  57.6 32.7 all-gather.7
  92.4 44.7 all-gather.9
  139.5 33.9 all-gather.11
